TPU v7x, 32 devices: a whole 2x2x4 slice. The times are simulated.
32 devices in a mesh: ta: 4 (over z), tp: 8 (over y, x, core).
Axes of the slice: x: 2, y: 2, z: 4, core: 2. Of those that a mesh axis runs over, the one named last changes fastest.
Arguments:
- lesser_history: bfloat16 [8, 8, 256, 512], P('ta', 'tp'), as said below
- greater_history: bfloat16 [8, 8, 256, 512], P('ta', 'tp'), as said below
- newest_lesser_row: bfloat16 [8, 256, 512], P('tp'), may hold values from -4 to 4
- newest_greater_row: bfloat16 [8, 256, 512], P('tp'), may hold values from -4 to 4
- propagator: bfloat16 [256, 512], replicated
Outputs:
- row_less_out: bfloat16 [8, 256, 512], P('tp')
- row_great_out: bfloat16 [8, 256, 512], P('tp')
Inputs may be any that keep to these rules, and one draw needn't show every extreme that they name: lesser_history[t', t] is minus the conjugate transpose of lesser_history[t, t'] for all stored times: its real part is the negated transpose, its imaginary part the transpose. greater_history[t', t] is minus the conjugate transpose of greater_history[t, t'] for all stored times.
All inputs are finite; a program needn't handle non-finite values.
Results may differ from a plain program's by a relative error of at most 0.012.
Values may be sent and summed in bfloat16 or wider, within the bound.
A program may use at most 64 MiB of HBM per device.

v0:
```python
import jax
import jax.numpy as jnp
from jax import lax
from jax.sharding import PartitionSpec as P

STEPS = 2


time_increment = 0.3


def spread(value, axis, source):
    kept = jnp.where(lax.axis_index(axis) == source, value, 0).astype(value.dtype)
    return lax.psum(kept, axis)


def split_complex_parts(tiles):
    width = tiles.shape[-2]
    return (tiles[..., :width], tiles[..., width:])


def self_energy(row_l, row_g):
    less_real, less_imag = split_complex_parts(row_l.astype(jnp.float32))
    great_real, great_imag = split_complex_parts(row_g.astype(jnp.float32))
    lsq_real = less_real * less_real - less_imag * less_imag
    lsq_imag = 2.0 * less_real * less_imag
    gsq_real = great_real * great_real - great_imag * great_imag
    gsq_imag = 2.0 * great_real * great_imag
    sigma_lesser = jnp.concatenate(
        [
            -(lsq_real * great_real + lsq_imag * great_imag),
            -(lsq_imag * great_real - lsq_real * great_imag),
        ],
        -1,
    )
    sigma_greater = jnp.concatenate(
        [
            -(gsq_real * less_real + gsq_imag * less_imag),
            -(gsq_imag * less_real - gsq_real * less_imag),
        ],
        -1,
    )
    sigma_retarded = sigma_greater - sigma_lesser
    return (
        sigma_lesser.astype(jnp.bfloat16),
        sigma_greater.astype(jnp.bfloat16),
        sigma_retarded.astype(jnp.bfloat16),
    )


def adjoint_sum(sigma, stored):
    width = sigma.shape[-2]
    sig_real, sig_imag = split_complex_parts(sigma)
    upper = jnp.concatenate([sig_real, sig_imag], -1)
    lower = jnp.concatenate([sig_imag, -sig_real], -1)
    stacked = jnp.concatenate([upper, lower], 1)
    result = jnp.einsum("cxk,rcyk->rxy", stacked, stored, preferred_element_type=jnp.float32)
    return jnp.concatenate([result[:, :width], result[:, width:]], -1)


def combine_blocks(result, width):
    real = result[:, :width, :width] - result[:, width:, width:]
    imag = result[:, :width, width:] + result[:, width:, :width]
    return jnp.concatenate([real, imag], -1)


def rotate_phase(collision_term):
    collision_real, collision_imaginary = split_complex_parts(collision_term)
    return jnp.concatenate(
        [time_increment * collision_imaginary, -time_increment * collision_real], -1
    )


def advance_rows(propagator, mixed_term):
    width = propagator.shape[0]
    prop_real, prop_imag = split_complex_parts(propagator)
    stacked = jnp.concatenate([prop_real, prop_imag], 0)
    result = jnp.einsum("xk,tky->txy", stacked, mixed_term, preferred_element_type=jnp.float32)
    return combine_blocks(result, width).astype(jnp.bfloat16)


def local(lesser_history, greater_history, newest_lesser_row, newest_greater_row, propagator):
    row_tiles = lesser_history.shape[0]
    column_tiles = lesser_history.shape[1]
    row_first = lax.axis_index("ta") * row_tiles
    column_first = lax.axis_index("tp") * column_tiles
    row_ids = row_first + jnp.arange(row_tiles, dtype=jnp.int32)
    column_ids = column_first + jnp.arange(column_tiles, dtype=jnp.int32)
    diff = (greater_history.astype(jnp.float32) - lesser_history.astype(jnp.float32)).astype(
        jnp.bfloat16
    )
    blank = jnp.zeros_like(diff)
    below = (column_ids[None, :] < row_ids[:, None])[:, :, None, None]
    difference_below = jnp.where(below, diff, blank)
    owner = column_first // row_tiles
    offset = jnp.clip(column_first - owner * row_tiles, 0, row_tiles - column_tiles)
    inside = owner == lax.axis_index("ta")
    for step in range(STEPS):
        sigma_lesser, sigma_greater, sigma_retarded = self_energy(
            newest_lesser_row, newest_greater_row
        )
        collision_lesser = adjoint_sum(sigma_lesser, difference_below) - adjoint_sum(
            sigma_retarded, lesser_history
        )
        collision_greater = adjoint_sum(sigma_greater, difference_below) - adjoint_sum(
            sigma_retarded, greater_history
        )
        base = jnp.zeros((row_tiles,) + newest_lesser_row.shape[1:], jnp.float32)
        local_lesser = lax.dynamic_update_slice_in_dim(
            base, newest_lesser_row.astype(jnp.float32), offset, 0
        )
        local_greater = lax.dynamic_update_slice_in_dim(
            base, newest_greater_row.astype(jnp.float32), offset, 0
        )
        local_lesser = jnp.where(inside, local_lesser, base)
        local_greater = jnp.where(inside, local_greater, base)
        mixed_lesser, mixed_greater = lax.psum(
            (
                rotate_phase(collision_lesser) + local_lesser,
                rotate_phase(collision_greater) + local_greater,
            ),
            "tp",
        )
        picked = jnp.stack(
            [
                lax.dynamic_slice_in_dim(mixed_lesser, offset, column_tiles, 0),
                lax.dynamic_slice_in_dim(mixed_greater, offset, column_tiles, 0),
            ]
        ).astype(jnp.bfloat16)
        arrived = spread(picked, "ta", owner)
        newest_lesser_row = advance_rows(propagator, arrived[0])
        newest_greater_row = advance_rows(propagator, arrived[1])
    return (newest_lesser_row, newest_greater_row)


def solution(mesh):
    placed = (
        P("ta", "tp", None, None),
        P("ta", "tp", None, None),
        P("tp", None, None),
        P("tp", None, None),
        P(),
    )
    return jax.shard_map(
        local,
        mesh=mesh,
        in_specs=placed,
        out_specs=(P("tp", None, None), P("tp", None, None)),
        check_vma=False,
    )
```

profile of v0, /device:TPU:0, one launch (start us, length us, event | category | flops | bytes accessed | tf_op | source)
XLA Modules:
  0.0 226.9 jit_solution(12655989336438470283)
XLA Ops:
  7.2 1.0 convert_element_type.179
  8.8 1.0 copy-done.2
  10.3 0.6 copy-done.3
  10.8 0.5 convolution_bitcast_fusion.10
  11.6 0.5 convolution_bitcast_fusion.11
  13.7 0.8 copy-done
  14.8 58.5 %all-reduce.10 = (bf16[2,256,512]{2,1,0:T(8,128)(2,1)}, bf16[2,256,512]{2,1,0:T(8,128)(2,1)}) all-reduce(f32[2,256,512]{2,1,0:T(8,128)S(1)} %fusion.10, f32[2,256,512]{2,1,0:T(8,128)S(1)} %fusion.13), channel_id=1, replica_groups=mesh['ta'=4,'tp'=8] {'tp'}, use_global_device_ids=true, to_apply=%region_1.2 | all-reduce | flops 524288 | bytes 3145728 | tf_op jit(solution)/shard_map/psum | solution.py:117
  73.3 1.0 fusion.39
  74.5 0.9 maximum_select_fusion
  75.4 0.9 copy-done.8
  76.3 37.8 %all-reduce.7.cloned.1.call-done = bf16[2,1,256,512]{3,2,1,0:T(8,128)(2,1)} async-done(((bf16[2,1,256,512]{3,2,1,0:T(8,128)(2,1)}), bf16[2,1,256,512]{3,2,1,0:T(8,128)(2,1)}) %all-reduce.7.cloned.1.call-update) | async-done | bytes 524304 | tf_op jit(solution)/shard_map/psum | solution.py:14
  114.1 1.2 convolution_bitcast_fusion
  115.5 1.0 copy-done.7
  117.3 0.5 convolution_bitcast_fusion.4
  117.8 0.5 convolution_bitcast_fusion.6
  118.3 1.0 copy-done.5
  119.3 0.5 convolution_bitcast_fusion.5
  119.9 0.5 convolution_bitcast_fusion.7
  121.6 57.3 %all-reduce.11 = (bf16[2,256,512]{2,1,0:T(8,128)(2,1)S(1)}, bf16[2,256,512]{2,1,0:T(8,128)(2,1)S(1)}) all-reduce(f32[2,256,512]{2,1,0:T(8,128)S(1)} %fusion.4, f32[2,256,512]{2,1,0:T(8,128)S(1)} %fusion.7), channel_id=1, replica_groups=mesh['ta'=4,'tp'=8] {'tp'}, use_global_device_ids=true, to_apply=%region_4.5 | all-reduce | flops 524288 | bytes 3145728 | tf_op jit(solution)/shard_map/psum | solution.py:117
  178.9 0.9 maximum_select_fusion.1
  179.8 36.6 %all-reduce.9.cloned.1.call-done = bf16[2,1,256,512]{3,2,1,0:T(8,128)(2,1)} async-done(((bf16[2,1,256,512]{3,2,1,0:T(8,128)(2,1)}), bf16[2,1,256,512]{3,2,1,0:T(8,128)(2,1)}) %all-reduce.9.cloned.1.call-update) | async-done | bytes 524304 | tf_op jit(solution)/shard_map/psum | solution.py:14
  216.4 1.3 convolution_bitcast_fusion.2
  217.8 0.8 copy.18
  219.3 0.8 copy.17
  (74 shorter events, 6.1 us)
Async XLA Ops:
  7.2 107.0 %all-reduce.7.cloned.1.call-start = ((), (), s32[]{:S(2)}) async-start(), calls=%async_computation | async-start | bytes 1048576 | tf_op jit(solution)/shard_map/psum | solution.py:14
  7.2 1.1 copy-start.1
  8.7 1.0 copy-start.2
  9.8 1.0 copy-start.3
  11.5 0.8 copy-start.4
  13.6 1.0 copy-start
  73.3 1.1 copy-start.9
  75.3 0.9 copy-start.8
  75.4 141.0 %all-reduce.9.cloned.1.call-start = ((), (), s32[]{:S(2)}) async-start(), calls=%async_computation.1 | async-start | bytes 1048576 | tf_op jit(solution)/shard_map/psum | solution.py:14
  115.4 1.0 copy-start.7
  118.3 1.0 copy-start.5
  217.8 1.0 copy-start.6
Sparse Core Ops, SparseCore 0:
  75.5 38.6 all-reduce.6
  179.9 36.4 all-reduce.8
where the time goes:
time: 227 us
  blocking collectives  116 us (51%)
  waiting for transfers between devices  74.5 us (33%)
  between operations  14.6 us (6%)
  local copies, waits for them, and re-layouts  9.06 us (4%)
  matrix products  6.9 us (3%)
  other arithmetic  6.05 us (3%)
    psum x2, blocking collectives, local(): lax.psum((rotate_phase(collision_lesser) + local_lesser, rotate_phase(col...  116 us
    psum x2, waiting for transfers between devices, spread(): return lax.psum(kept, axis)  74.4 us
    unnamed x22, local copies, waits for them, and re-layouts  7.33 us
  transfers between devices with their start and end apart: 2, of which 2 were waited for; matrix products, arithmetic and copies ran while one was open for 0% of the time, Pallas kernels for 0%

commit v1 on v0

v1 whole, which is shorter than its diff:
```python
import jax
import jax.numpy as jnp
from jax import lax
from jax.experimental import pallas as pl
from jax.experimental.pallas import tpu as pltpu
from jax.sharding import PartitionSpec as P

time_increment = 0.3
MESH = pl.DeviceIdType.MESH
f32 = jnp.float32
bf16 = jnp.bfloat16


def self_energy(row_l, row_g):
    w = row_l.shape[-1] // 2
    lr, li = row_l[:, :w].astype(f32), row_l[:, w:].astype(f32)
    gr, gi = row_g[:, :w].astype(f32), row_g[:, w:].astype(f32)
    lsr, lsi = lr * lr - li * li, 2.0 * lr * li
    gsr, gsi = gr * gr - gi * gi, 2.0 * gr * gi
    less = (-(lsr * gr + lsi * gi), -(lsi * gr - lsr * gi))
    great = (-(gsr * lr + gsi * li), -(gsi * lr - gsr * li))
    return less, great


def factors(row_l, row_g, below):
    (lr, li), (gr, gi) = self_energy(row_l, row_g)
    on_l = (jnp.where(below, gr, gr - lr), jnp.where(below, gi, gi - li))
    on_g = (jnp.where(below, -lr, gr - lr), jnp.where(below, -li, gi - li))
    return on_l, on_g


def complex_square(tile):
    w = tile.shape[0]
    re, im = tile[:, :w], tile[:, w:]
    return jnp.concatenate(
        [jnp.concatenate([re, im], 1), jnp.concatenate([-im, re], 1)], 0
    )


def rotate(coll):
    w = coll.shape[-1] // 2
    return jnp.concatenate(
        [time_increment * coll[:, w:], -time_increment * coll[:, :w]], 1
    )


def kernel(
    na,
    nt,
    less_ref,
    great_ref,
    rowl_ref,
    rowg_ref,
    prop_ref,
    outl_ref,
    outg_ref,
    part,
    sib_in,
    pre,
    rs_in,
    gath,
    zpart,
    zin,
    zg,
    stored_l,
    stored_g,
    sib_s,
    sib_r,
    rs_s,
    rs_r,
    ag_s,
    ag_r,
    fw_s,
    fw_r,
    zr_s,
    zr_r,
    za_s,
    za_r,
):
    nq = nt // 2
    w = prop_ref.shape[0]
    br = w // nq
    a = lax.axis_index("ta")
    c = lax.axis_index("tp")
    q = c // 2
    h = c - 2 * q
    other = 1 - h
    sib = 2 * q + other

    barrier = pltpu.get_barrier_semaphore()
    pl.semaphore_signal(barrier, inc=1, device_id={"tp": sib}, device_id_type=MESH)
    for k in range(1, nq):
        to = 2 * lax.rem(q + k, nq) + h
        pl.semaphore_signal(barrier, inc=1, device_id={"tp": to}, device_id_type=MESH)
    for k in range(1, na):
        to = lax.rem(a + k, na)
        pl.semaphore_signal(barrier, inc=1, device_id={"ta": to}, device_id_type=MESH)

    def remote(src, dst, ss, rs, **to):
        return pltpu.make_async_remote_copy(
            src_ref=src, dst_ref=dst, send_sem=ss, recv_sem=rs, device_id=to, device_id_type=MESH
        )

    row_l, row_g = rowl_ref[0], rowg_ref[0]
    prop = prop_ref[...]
    for i in range(2):
        r = 2 * a + i
        below = c < r
        on_l, on_g = factors(row_l, row_g, below)
        prods = []
        for (re, im), stored in ((on_l, less_ref), (on_g, great_ref)):
            re, im = re.astype(bf16), im.astype(bf16)
            lhs = jnp.concatenate(
                [jnp.concatenate([-im, re], 1), jnp.concatenate([re, im], 1)], 0
            )
            res = lax.dot_general(
                lhs, stored[i, 0], (((1,), (1,)), ((), ())), preferred_element_type=f32
            )
            prods.append(jnp.concatenate([res[:w], res[w:]], 1) * time_increment)
        both = jnp.where(below, 1.0, 0.0).astype(f32)
        mine = jnp.where(c == r, 1.0, 0.0).astype(f32)
        for kind in range(2):
            row = (row_l, row_g)[kind].astype(f32)
            mixed = prods[kind] + both * prods[1 - kind] + mine * row
            new = jnp.dot(prop, complex_square(mixed.astype(bf16)), preferred_element_type=f32)
            new = new.astype(bf16)
            for g in range(nq):
                part[g, i, kind] = new[g * br : (g + 1) * br]

    pl.semaphore_wait(barrier, nq + na - 1)

    order = [k % nq for k in range(1, nq + 1)]
    sends = []
    for k in order:
        g = lax.rem(q + k, nq)
        cp = remote(part.at[g, other], sib_in.at[k], sib_s.at[k], sib_r.at[k], tp=sib)
        cp.start()
        sends.append(cp)

    for i in range(2):
        stored_l[i] = complex_square(less_ref[i, 0])
        stored_g[i] = complex_square(great_ref[i, 0])

    rs = {}
    for k in order:
        g = lax.rem(q + k, nq)
        remote(part.at[g, other], sib_in.at[k], sib_s.at[k], sib_r.at[k], tp=sib).wait_recv()
        total = part[g, h].astype(f32) + sib_in[k].astype(f32)
        if k:
            pre[k] = total.astype(bf16)
            cp = remote(pre.at[k], rs_in.at[k], rs_s.at[k], rs_r.at[k], tp=2 * g + h)
            cp.start()
            rs[k] = cp
            sends.append(cp)
    for k in range(1, nq):
        rs[k].wait_recv()
        total = total + rs_in[k].astype(f32)
    gath[q, h] = total.astype(bf16)

    ag = {}
    for k in range(1, nq):
        g = lax.rem(q + k, nq)
        cp = remote(gath.at[q, h], gath.at[q, h], ag_s.at[k], ag_r.at[k], tp=2 * g + h)
        cp.start()
        ag[k] = cp
        sends.append(cp)

    def forward(g, k, half):
        return remote(gath.at[g, half], gath.at[g, half], fw_s.at[k], fw_r.at[k], tp=sib)

    cp = forward(q, 0, h)
    cp.start()
    sends.append(cp)

    for k in range(nq):
        g = lax.rem(q - k + nq, nq)
        if k:
            remote(gath.at[g, h], gath.at[g, h], ag_s.at[k], ag_r.at[k], tp=sib).wait_recv()
            cp = forward(g, k, h)
            cp.start()
            sends.append(cp)
        forward(g, k, other).wait_recv()

        colls = [jnp.zeros((br, 2 * w), f32), jnp.zeros((br, 2 * w), f32)]
        for i in range(2):
            below = 2 * a + i < c
            both = jnp.where(below, 1.0, 0.0).astype(f32)
            on_l, on_g = factors(gath[g, i, 0], gath[g, i, 1], below)
            prods = []
            for (re, im), stored in ((on_l, stored_l), (on_g, stored_g)):
                lhs = jnp.concatenate([re, im], 1).astype(bf16)
                prods.append(jnp.dot(lhs, stored[i], preferred_element_type=f32))
            for kind in range(2):
                colls[kind] = colls[kind] + prods[kind] + both * prods[1 - kind]
        mine = jnp.where(q == a, 1.0, 0.0).astype(f32)
        for kind in range(2):
            mixed = rotate(colls[kind]) + mine * gath[g, h, kind].astype(f32)
            zpart[g, kind] = mixed.astype(bf16)

        @pl.when(g != a)
        def _():
            remote(zpart.at[g], zin.at[a], zr_s.at[g], zr_r.at[a], ta=g).start()

    total = zpart[a].astype(f32)
    for j in range(1, na):
        b = lax.rem(a + j, na)
        remote(zpart.at[b], zin.at[b], zr_s.at[b], zr_r.at[b], ta=b).wait_recv()
        total = total + zin[b].astype(f32)
    zg[a] = total.astype(bf16)

    for j in range(1, na):
        b = lax.rem(a + j, na)
        cp = remote(zg.at[a], zg.at[a], za_s.at[j], za_r.at[j], ta=b)
        cp.start()
        sends.append(cp)
    for j in range(1, na):
        b = lax.rem(a - j + na, na)
        remote(zg.at[b], zg.at[b], za_s.at[j], za_r.at[j], ta=b).wait_recv()
    for kind, out in ((0, outl_ref), (1, outg_ref)):
        mixed = jnp.concatenate([zg[b, kind] for b in range(na)], 0)
        out[0] = jnp.dot(prop, complex_square(mixed), preferred_element_type=f32).astype(bf16)

    for cp in sends:
        cp.wait_send()
    for j in range(1, na):
        b = lax.rem(a + j, na)
        remote(zpart.at[b], zin.at[b], zr_s.at[b], zr_r.at[b], ta=b).wait_send()


def solution(mesh):
    na, nt = mesh.shape["ta"], mesh.shape["tp"]
    nq = nt // 2

    def local(less, great, rowl, rowg, prop):
        w = prop.shape[0]
        br = w // nq
        chunk = (2, br, 2 * w)
        dma = pltpu.SemaphoreType.DMA
        out = jax.ShapeDtypeStruct(rowl.shape, rowl.dtype)
        return pl.pallas_call(
            lambda *refs: kernel(na, nt, *refs),
            out_shape=(out, out),
            in_specs=[pl.BlockSpec(memory_space=pltpu.VMEM)] * 5,
            out_specs=(pl.BlockSpec(memory_space=pltpu.VMEM),) * 2,
            scratch_shapes=[
                pltpu.VMEM((nq, 2) + chunk, bf16),
                pltpu.VMEM((nq,) + chunk, bf16),
                pltpu.VMEM((nq,) + chunk, bf16),
                pltpu.VMEM((nq,) + chunk, bf16),
                pltpu.VMEM((nq, 2) + chunk, bf16),
                pltpu.VMEM((na,) + chunk, bf16),
                pltpu.VMEM((na,) + chunk, bf16),
                pltpu.VMEM((na,) + chunk, bf16),
                pltpu.VMEM((2, 2 * w, 2 * w), bf16),
                pltpu.VMEM((2, 2 * w, 2 * w), bf16),
            ]
            + [dma((nq,))] * 8
            + [dma((na,))] * 4,
            compiler_params=pltpu.CompilerParams(
                collective_id=0, has_side_effects=True, vmem_limit_bytes=48 * 1024 * 1024
            ),
            name="advance",
        )(less, great, rowl, rowg, prop)

    placed = (
        P("ta", "tp", None, None),
        P("ta", "tp", None, None),
        P("tp", None, None),
        P("tp", None, None),
        P(),
    )
    return jax.shard_map(
        local,
        mesh=mesh,
        in_specs=placed,
        out_specs=(P("tp", None, None), P("tp", None, None)),
        check_vma=False,
    )
```

time: 227 us -> 56.5 us (0.25)
  the two profiles are of different devices: /device:TPU:0 before, /device:TPU:30 now
where the time goes in v1:
time: 56.5 us; the launch traced here: 56.2 us
  Pallas kernels  49.3 us (87%)
  local copies, waits for them, and re-layouts  6.33 us (11%)
  between operations  0.65 us (1%)
    pallas_call x1, Pallas kernels, local(): pl.pallas_call(lambda *refs: kernel(na, nt, *refs), out_shape=(out, out),...  49.3 us
    unnamed x12, local copies, waits for them, and re-layouts  6.33 us

profile of v1, /device:TPU:30, one launch (start us, length us, event | category | flops | bytes accessed | tf_op | source)
XLA Modules:
  0.0 56.2 jit_solution(12907711665421705968)
XLA Ops:
  0.6 0.0 copy-start
  0.6 1.0 %copy-done = bf16[2,1,256,512]{3,2,1,0:T(8,128)(2,1)S(1)} copy-done((bf16[2,1,256,512]{3,2,1,0:T(8,128)(2,1)S(1)}, bf16[2,1,256,512]{3,2,1,0:T(8,128)(2,1)}, u32[]{:S(2)}) %copy-start) | copy-done | bytes 524312
  1.7 0.0 copy-start.1
  1.7 1.0 %copy-done.1 = bf16[2,1,256,512]{3,2,1,0:T(8,128)(2,1)S(1)} copy-done((bf16[2,1,256,512]{3,2,1,0:T(8,128)(2,1)S(1)}, bf16[2,1,256,512]{3,2,1,0:T(8,128)(2,1)}, u32[]{:S(2)}) %copy-start.1) | copy-done | bytes 524312
  2.7 0.0 copy-start.2
  2.7 0.9 %copy-done.2 = bf16[1,256,512]{2,1,0:T(8,128)(2,1)S(1)} copy-done((bf16[1,256,512]{2,1,0:T(8,128)(2,1)S(1)}, bf16[1,256,512]{2,1,0:T(8,128)(2,1)}, u32[]{:S(2)}) %copy-start.2) | copy-done | bytes 262168
  3.7 0.0 copy-start.3
  3.7 0.9 %copy-done.3 = bf16[1,256,512]{2,1,0:T(8,128)(2,1)S(1)} copy-done((bf16[1,256,512]{2,1,0:T(8,128)(2,1)S(1)}, bf16[1,256,512]{2,1,0:T(8,128)(2,1)}, u32[]{:S(2)}) %copy-start.3) | copy-done | bytes 262168
  4.6 0.0 copy-start.4
  4.6 0.9 %copy-done.4 = bf16[256,512]{1,0:T(8,128)(2,1)S(1)} copy-done((bf16[256,512]{1,0:T(8,128)(2,1)S(1)}, bf16[256,512]{1,0:T(8,128)(2,1)}, u32[]{:S(2)}) %copy-start.4) | copy-done | bytes 262168
  5.6 49.3 %advance.1 = (bf16[1,256,512]{2,1,0:T(8,128)(2,1)S(1)}, bf16[1,256,512]{2,1,0:T(8,128)(2,1)S(1)}) custom-call(bf16[2,1,256,512]{3,2,1,0:T(8,128)(2,1)S(1)} %copy-done, bf16[2,1,256,512]{3,2,1,0:T(8,128)(2,1)S(1)} %copy-done.1, bf16[1,256,512]{2,1,0:T(8,128)(2,1)S(1)} %copy-done.2, bf16[1,256,512]{2,1,0:T(8,128)(2,1)S(1)} %copy-done.3, ...), custom_call_target="tpu_custom_call" | custom-call | tf_op jit(solution)/shard_map/advance/pallas_call | solution.py:240
  54.8 0.7 %copy.9 = bf16[1,256,512]{2,1,0:T(8,128)(2,1)} copy(bf16[1,256,512]{2,1,0:T(8,128)(2,1)S(1)} %get-tuple-element.4) | data formatting | bytes 524288
  55.5 0.7 %copy.10 = bf16[1,256,512]{2,1,0:T(8,128)(2,1)} copy(bf16[1,256,512]{2,1,0:T(8,128)(2,1)S(1)} %get-tuple-element.5) | data formatting | bytes 524288
Async XLA Ops:
  0.6 1.0 %copy-start = (bf16[2,1,256,512]{3,2,1,0:T(8,128)(2,1)S(1)}, bf16[2,1,256,512]{3,2,1,0:T(8,128)(2,1)}, u32[]{:S(2)}) copy-start(bf16[2,1,256,512]{3,2,1,0:T(8,128)(2,1)} %refs_0_.1) | copy-start | bytes 1572868
  1.7 1.0 %copy-start.1 = (bf16[2,1,256,512]{3,2,1,0:T(8,128)(2,1)S(1)}, bf16[2,1,256,512]{3,2,1,0:T(8,128)(2,1)}, u32[]{:S(2)}) copy-start(bf16[2,1,256,512]{3,2,1,0:T(8,128)(2,1)} %refs_1_.1) | copy-start | bytes 1572868
  2.7 0.9 %copy-start.2 = (bf16[1,256,512]{2,1,0:T(8,128)(2,1)S(1)}, bf16[1,256,512]{2,1,0:T(8,128)(2,1)}, u32[]{:S(2)}) copy-start(bf16[1,256,512]{2,1,0:T(8,128)(2,1)} %refs_2_.1) | copy-start | bytes 786436
  3.7 0.9 %copy-start.3 = (bf16[1,256,512]{2,1,0:T(8,128)(2,1)S(1)}, bf16[1,256,512]{2,1,0:T(8,128)(2,1)}, u32[]{:S(2)}) copy-start(bf16[1,256,512]{2,1,0:T(8,128)(2,1)} %refs_3_.1) | copy-start | bytes 786436
  4.6 0.9 %copy-start.4 = (bf16[256,512]{1,0:T(8,128)(2,1)S(1)}, bf16[256,512]{1,0:T(8,128)(2,1)}, u32[]{:S(2)}) copy-start(bf16[256,512]{1,0:T(8,128)(2,1)} %refs_4_.1) | copy-start | bytes 786436

commit v2 on v1

v2 whole, which is shorter than its diff:
```python
import jax
import jax.numpy as jnp
from jax import lax
from jax.experimental import pallas as pl
from jax.experimental.pallas import tpu as pltpu
from jax.sharding import PartitionSpec as P

time_increment = 0.3
MESH = pl.DeviceIdType.MESH
f32 = jnp.float32
bf16 = jnp.bfloat16


def self_energy(row_l, row_g):
    w = row_l.shape[-1] // 2
    lr, li = row_l[:, :w].astype(f32), row_l[:, w:].astype(f32)
    gr, gi = row_g[:, :w].astype(f32), row_g[:, w:].astype(f32)
    lsr, lsi = lr * lr - li * li, 2.0 * lr * li
    gsr, gsi = gr * gr - gi * gi, 2.0 * gr * gi
    less = (-(lsr * gr + lsi * gi), -(lsi * gr - lsr * gi))
    great = (-(gsr * lr + gsi * li), -(gsi * lr - gsr * li))
    return less, great


def factors(row_l, row_g, below):
    (lr, li), (gr, gi) = self_energy(row_l, row_g)
    on_l = (jnp.where(below, gr, gr - lr), jnp.where(below, gi, gi - li))
    on_g = (jnp.where(below, -lr, gr - lr), jnp.where(below, -li, gi - li))
    return on_l, on_g


def complex_square(tile):
    w = tile.shape[0]
    re, im = tile[:, :w], tile[:, w:]
    return jnp.concatenate(
        [jnp.concatenate([re, im], 1), jnp.concatenate([-im, re], 1)], 0
    )


def rotate(coll):
    w = coll.shape[-1] // 2
    return jnp.concatenate(
        [time_increment * coll[:, w:], -time_increment * coll[:, :w]], 1
    )


def kernel(
    na,
    nt,
    nu,
    less_hbm,
    great_hbm,
    rowl_hbm,
    rowg_hbm,
    prop_hbm,
    outl_ref,
    outg_ref,
    less_ref,
    great_ref,
    rows_ref,
    prop_ref,
    part,
    sib_in,
    pre,
    rs_in,
    gath,
    zpart,
    zsib,
    zpre,
    zin,
    zg,
    stored_l,
    stored_g,
    load,
    sib_s,
    sib_r,
    rs_s,
    rs_r,
    ag_s,
    ag_r,
    fw_s,
    fw_r,
    zs_s,
    zs_r,
    zr_s,
    zr_r,
    za_s,
    za_r,
    zf_s,
    zf_r,
):
    nq = nt // 2
    npair = na // 2
    w = prop_ref.shape[0]
    wu = w // nu
    br = wu // nq
    a = lax.axis_index("ta")
    c = lax.axis_index("tp")
    q = c // 2
    h = c - 2 * q
    other = 1 - h
    sib = 2 * q + other
    pa = a // 2
    ha = a - 2 * pa
    zsibling = 2 * pa + 1 - ha

    def fetch(src, dst, n):
        return pltpu.make_async_copy(src, dst, load.at[n])

    loads = [
        fetch(rowl_hbm.at[0], rows_ref.at[0], 0),
        fetch(rowg_hbm.at[0], rows_ref.at[1], 1),
        fetch(less_hbm.at[other, 0], less_ref.at[other], 2),
        fetch(great_hbm.at[other, 0], great_ref.at[other], 3),
        fetch(prop_hbm, prop_ref, 4),
        fetch(less_hbm.at[h, 0], less_ref.at[h], 5),
        fetch(great_hbm.at[h, 0], great_ref.at[h], 6),
    ]
    for cp in loads:
        cp.start()

    barrier = pltpu.get_barrier_semaphore()
    pl.semaphore_signal(barrier, inc=1, device_id={"tp": sib}, device_id_type=MESH)
    for k in range(1, nq):
        to = 2 * lax.rem(q + k, nq) + h
        pl.semaphore_signal(barrier, inc=1, device_id={"tp": to}, device_id_type=MESH)
    pl.semaphore_signal(barrier, inc=1, device_id={"ta": zsibling}, device_id_type=MESH)
    for k in range(1, npair):
        to = 2 * lax.rem(pa + k, npair) + ha
        pl.semaphore_signal(barrier, inc=1, device_id={"ta": to}, device_id_type=MESH)

    def remote(src, dst, ss, rs, **to):
        return pltpu.make_async_remote_copy(
            src_ref=src, dst_ref=dst, send_sem=ss, recv_sem=rs, device_id=to, device_id_type=MESH
        )

    sends = []

    def launch(cp):
        cp.start()
        sends.append(cp)

    loads[0].wait()
    loads[1].wait()
    row_l, row_g = rows_ref[0], rows_ref[1]
    (lr, li), (gr, gi) = self_energy(row_l, row_g)

    def first(i):
        r = 2 * a + i
        below = c < r
        on_l = (jnp.where(below, gr, gr - lr), jnp.where(below, gi, gi - li))
        on_g = (jnp.where(below, -lr, gr - lr), jnp.where(below, -li, gi - li))
        prods = []
        for (re, im), stored in ((on_l, less_ref), (on_g, great_ref)):
            re, im = re.astype(bf16), im.astype(bf16)
            lhs = jnp.concatenate(
                [jnp.concatenate([-im, re], 1), jnp.concatenate([re, im], 1)], 0
            )
            res = lax.dot_general(
                lhs, stored[i], (((1,), (1,)), ((), ())), preferred_element_type=f32
            )
            prods.append(jnp.concatenate([res[:w], res[w:]], 1) * time_increment)
        both = jnp.where(below, 1.0, 0.0).astype(f32)
        mine = jnp.where(c == r, 1.0, 0.0).astype(f32)
        for kind in range(2):
            row = (row_l, row_g)[kind].astype(f32)
            mixed = prods[kind] + both * prods[1 - kind] + mine * row
            new = jnp.dot(
                prop_ref[...], complex_square(mixed.astype(bf16)), preferred_element_type=f32
            )
            new = new.astype(bf16)
            for u in range(nu):
                for g in range(nq):
                    at = u * wu + g * br
                    part[g, i, u, kind] = new[at : at + br]

    for n in (2, 3, 4):
        loads[n].wait()
    first(other)

    pl.semaphore_wait(barrier, nq + npair)

    order = [k % nq for k in range(1, nq + 1)]

    def to_sibling(k, u):
        g = lax.rem(q + k, nq)
        return remote(part.at[g, other, u], sib_in.at[k, u], sib_s.at[k, u], sib_r.at[k, u], tp=sib)

    for u in range(nu):
        for k in order:
            launch(to_sibling(k, u))
    loads[5].wait()
    loads[6].wait()
    first(h)

    def scatter(k, u):
        g = lax.rem(q + k, nq)
        return remote(pre.at[k, u], rs_in.at[k, u], rs_s.at[k, u], rs_r.at[k, u], tp=2 * g + h)

    kept = []
    for u in range(nu):
        for k in order:
            g = lax.rem(q + k, nq)
            to_sibling(k, u).wait_recv()
            total = part[g, h, u].astype(f32) + sib_in[k, u].astype(f32)
            if k:
                pre[k, u] = total.astype(bf16)
                launch(scatter(k, u))
            else:
                kept.append(total)

    for i in range(2):
        stored_l[i] = complex_square(less_ref[i])
        stored_g[i] = complex_square(great_ref[i])

    def gather(k, u):
        g = lax.rem(q + k, nq)
        return remote(gath.at[q, h, u], gath.at[q, h, u], ag_s.at[k, u], ag_r.at[k, u], tp=2 * g + h)

    def forward(k, u, half):
        g = lax.rem(q - k + nq, nq)
        return remote(gath.at[g, half, u], gath.at[g, half, u], fw_s.at[k, u], fw_r.at[k, u], tp=sib)

    for u in range(nu):
        total = kept[u]
        for k in range(1, nq):
            scatter(k, u).wait_recv()
            total = total + rs_in[k, u].astype(f32)
        gath[q, h, u] = total.astype(bf16)
        for k in range(1, nq):
            launch(gather(k, u))
        launch(forward(0, u, h))

    def z_sibling(pair, u):
        b = 2 * pair + 1 - ha
        return remote(zpart.at[b, u], zsib.at[pair, u], zs_s.at[pair, u], zs_r.at[pair, u], ta=zsibling)

    def second(k, u):
        g = lax.rem(q - k + nq, nq)
        forward(k, u, other).wait_recv()
        colls = [jnp.zeros((br, 2 * w), f32), jnp.zeros((br, 2 * w), f32)]
        for i in range(2):
            below = 2 * a + i < c
            both = jnp.where(below, 1.0, 0.0).astype(f32)
            on_l, on_g = factors(gath[g, i, u, 0], gath[g, i, u, 1], below)
            prods = []
            for (re, im), stored in ((on_l, stored_l), (on_g, stored_g)):
                lhs = jnp.concatenate([re, im], 1).astype(bf16)
                prods.append(jnp.dot(lhs, stored[i], preferred_element_type=f32))
            for kind in range(2):
                colls[kind] = colls[kind] + prods[kind] + both * prods[1 - kind]
        mine = jnp.where(q == a, 1.0, 0.0).astype(f32)
        for kind in range(2):
            mixed = rotate(colls[kind]) + mine * gath[g, h, u, kind].astype(f32)
            zpart[g, u, kind] = mixed.astype(bf16)
        pair = g // 2

        @pl.when(g - 2 * pair != ha)
        def _():
            z_sibling(pair, u).start()

    def z_scatter(k, u):
        b = 2 * lax.rem(pa + k, npair) + ha
        return remote(zpre.at[k, u], zin.at[k, u], zr_s.at[k, u], zr_r.at[k, u], ta=b)

    zkept = {}

    def z_pairs(u):
        for k in [k % npair for k in range(1, npair + 1)]:
            pair = lax.rem(pa + k, npair)
            z_sibling(pair, u).wait_recv()
            total = zpart[2 * pair + ha, u].astype(f32) + zsib[pair, u].astype(f32)
            if k:
                zpre[k, u] = total.astype(bf16)
                launch(z_scatter(k, u))
            else:
                zkept[u] = total

    def z_gather(k, u):
        b = 2 * lax.rem(pa + k, npair) + ha
        return remote(zg.at[a, u], zg.at[a, u], za_s.at[k, u], za_r.at[k, u], ta=b)

    def z_forward(k, u, half):
        b = 2 * lax.rem(pa - k + npair, npair) + half
        return remote(zg.at[b, u], zg.at[b, u], zf_s.at[k, u], zf_r.at[k, u], ta=zsibling)

    def z_finish(u):
        total = zkept[u]
        for k in range(1, npair):
            z_scatter(k, u).wait_recv()
            total = total + zin[k, u].astype(f32)
        zg[a, u] = total.astype(bf16)
        for k in range(1, npair):
            launch(z_gather(k, u))
        launch(z_forward(0, u, ha))

    for u in range(nu):
        for k in range(nq):
            if k:
                gather(k, u).wait_recv()
                launch(forward(k, u, h))
                second(k - 1, u)
            if u and k == nq // 2:
                z_pairs(u - 1)
        second(nq - 1, u)
        if u:
            z_finish(u - 1)
    z_pairs(nu - 1)
    z_finish(nu - 1)

    outs = [jnp.zeros((w, 2 * w), f32), jnp.zeros((w, 2 * w), f32)]
    for u in range(nu):
        for k in range(1, npair):
            z_gather(k, u).wait_recv()
            launch(z_forward(k, u, ha))
        for k in range(npair):
            z_forward(k, u, 1 - ha).wait_recv()
        at = u * wu
        left = jnp.concatenate(
            [prop_ref[:, at : at + wu], prop_ref[:, w + at : w + at + wu]], 1
        )
        for kind in range(2):
            mixed = jnp.concatenate([zg[b, u, kind] for b in range(na)], 0)
            re, im = mixed[:, :w], mixed[:, w:]
            right = jnp.concatenate(
                [jnp.concatenate([re, im], 1), jnp.concatenate([-im, re], 1)], 0
            )
            outs[kind] = outs[kind] + jnp.dot(left, right, preferred_element_type=f32)
    outl_ref[0] = outs[0].astype(bf16)
    outg_ref[0] = outs[1].astype(bf16)

    for cp in sends:
        cp.wait_send()
    for u in range(nu):
        for pair in range(npair):
            z_sibling(pair, u).wait_send()


def solution(mesh):
    na, nt = mesh.shape["ta"], mesh.shape["tp"]
    nq = nt // 2
    npair = na // 2

    def local(less, great, rowl, rowg, prop):
        w = prop.shape[0]
        nu = 2 if w // nq >= 32 else 1
        piece = (nu, 2, w // (nq * nu), 2 * w)
        dma = pltpu.SemaphoreType.DMA
        out = jax.ShapeDtypeStruct(rowl.shape, rowl.dtype)
        return pl.pallas_call(
            lambda *refs: kernel(na, nt, nu, *refs),
            out_shape=(out, out),
            in_specs=[pl.BlockSpec(memory_space=pltpu.HBM)] * 5,
            out_specs=(pl.BlockSpec(memory_space=pltpu.VMEM),) * 2,
            scratch_shapes=[
                pltpu.VMEM((2, w, 2 * w), bf16),
                pltpu.VMEM((2, w, 2 * w), bf16),
                pltpu.VMEM((2, w, 2 * w), bf16),
                pltpu.VMEM((w, 2 * w), bf16),
                pltpu.VMEM((nq, 2) + piece, bf16),
                pltpu.VMEM((nq,) + piece, bf16),
                pltpu.VMEM((nq,) + piece, bf16),
                pltpu.VMEM((nq,) + piece, bf16),
                pltpu.VMEM((nq, 2) + piece, bf16),
                pltpu.VMEM((na,) + piece, bf16),
                pltpu.VMEM((npair,) + piece, bf16),
                pltpu.VMEM((npair,) + piece, bf16),
                pltpu.VMEM((npair,) + piece, bf16),
                pltpu.VMEM((na,) + piece, bf16),
                pltpu.VMEM((2, 2 * w, 2 * w), bf16),
                pltpu.VMEM((2, 2 * w, 2 * w), bf16),
                dma((7,)),
            ]
            + [dma((nq, nu))] * 8
            + [dma((npair, nu))] * 8,
            compiler_params=pltpu.CompilerParams(
                collective_id=0, has_side_effects=True, vmem_limit_bytes=48 * 1024 * 1024
            ),
            name="advance",
        )(less, great, rowl, rowg, prop)

    placed = (
        P("ta", "tp", None, None),
        P("ta", "tp", None, None),
        P("tp", None, None),
        P("tp", None, None),
        P(),
    )
    return jax.shard_map(
        local,
        mesh=mesh,
        in_specs=placed,
        out_specs=(P("tp", None, None), P("tp", None, None)),
        check_vma=False,
    )
```

time: 56.5 us -> 51 us (0.903)
  the two profiles are of different devices: /device:TPU:30 before, /device:TPU:0 now
where the time goes in v2:
time: 51 us; the launch traced here: 50.7 us
  Pallas kernels  43.7 us (86%)
  local copies, waits for them, and re-layouts  6.33 us (12%)
  between operations  0.65 us (1%)
    pallas_call x1, Pallas kernels, local(): pl.pallas_call(lambda *refs: kernel(na, nt, nu, *refs), out_shape=(out, o...  43.7 us
    unnamed x12, local copies, waits for them, and re-layouts  6.33 us

profile of v2, /device:TPU:0, one launch (start us, length us, event | category | flops | bytes accessed | tf_op | source)
XLA Modules:
  0.0 50.7 jit_solution(1608277733030852632)
XLA Ops:
  0.6 0.0 copy-start
  0.6 1.0 %copy-done = bf16[2,1,256,512]{3,2,1,0:T(8,128)(2,1)S(1)} copy-done((bf16[2,1,256,512]{3,2,1,0:T(8,128)(2,1)S(1)}, bf16[2,1,256,512]{3,2,1,0:T(8,128)(2,1)}, u32[]{:S(2)}) %copy-start) | copy-done | bytes 524312
  1.7 0.0 copy-start.1
  1.7 1.0 %copy-done.1 = bf16[2,1,256,512]{3,2,1,0:T(8,128)(2,1)S(1)} copy-done((bf16[2,1,256,512]{3,2,1,0:T(8,128)(2,1)S(1)}, bf16[2,1,256,512]{3,2,1,0:T(8,128)(2,1)}, u32[]{:S(2)}) %copy-start.1) | copy-done | bytes 524312
  2.7 0.0 copy-start.2
  2.7 0.9 %copy-done.2 = bf16[1,256,512]{2,1,0:T(8,128)(2,1)S(1)} copy-done((bf16[1,256,512]{2,1,0:T(8,128)(2,1)S(1)}, bf16[1,256,512]{2,1,0:T(8,128)(2,1)}, u32[]{:S(2)}) %copy-start.2) | copy-done | bytes 262168
  3.7 0.0 copy-start.3
  3.7 0.9 %copy-done.3 = bf16[1,256,512]{2,1,0:T(8,128)(2,1)S(1)} copy-done((bf16[1,256,512]{2,1,0:T(8,128)(2,1)S(1)}, bf16[1,256,512]{2,1,0:T(8,128)(2,1)}, u32[]{:S(2)}) %copy-start.3) | copy-done | bytes 262168
  4.6 0.0 copy-start.4
  4.6 0.9 %copy-done.4 = bf16[256,512]{1,0:T(8,128)(2,1)S(1)} copy-done((bf16[256,512]{1,0:T(8,128)(2,1)S(1)}, bf16[256,512]{1,0:T(8,128)(2,1)}, u32[]{:S(2)}) %copy-start.4) | copy-done | bytes 262168
  5.6 43.7 %advance.1 = (bf16[1,256,512]{2,1,0:T(8,128)(2,1)S(1)}, bf16[1,256,512]{2,1,0:T(8,128)(2,1)S(1)}) custom-call(bf16[2,1,256,512]{3,2,1,0:T(8,128)(2,1)S(1)} %copy-done, bf16[2,1,256,512]{3,2,1,0:T(8,128)(2,1)S(1)} %copy-done.1, bf16[1,256,512]{2,1,0:T(8,128)(2,1)S(1)} %copy-done.2, bf16[1,256,512]{2,1,0:T(8,128)(2,1)S(1)} %copy-done.3, ...), custom_call_target="tpu_custom_call" | custom-call | tf_op jit(solution)/shard_map/advance/pallas_call | solution.py:350
  49.3 0.7 %copy.9 = bf16[1,256,512]{2,1,0:T(8,128)(2,1)} copy(bf16[1,256,512]{2,1,0:T(8,128)(2,1)S(1)} %get-tuple-element.4) | data formatting | bytes 524288
  50.0 0.7 %copy.10 = bf16[1,256,512]{2,1,0:T(8,128)(2,1)} copy(bf16[1,256,512]{2,1,0:T(8,128)(2,1)S(1)} %get-tuple-element.5) | data formatting | bytes 524288
Async XLA Ops:
  0.6 1.0 %copy-start = (bf16[2,1,256,512]{3,2,1,0:T(8,128)(2,1)S(1)}, bf16[2,1,256,512]{3,2,1,0:T(8,128)(2,1)}, u32[]{:S(2)}) copy-start(bf16[2,1,256,512]{3,2,1,0:T(8,128)(2,1)} %refs_0_.1) | copy-start | bytes 1572868
  1.7 1.0 %copy-start.1 = (bf16[2,1,256,512]{3,2,1,0:T(8,128)(2,1)S(1)}, bf16[2,1,256,512]{3,2,1,0:T(8,128)(2,1)}, u32[]{:S(2)}) copy-start(bf16[2,1,256,512]{3,2,1,0:T(8,128)(2,1)} %refs_1_.1) | copy-start | bytes 1572868
  2.7 0.9 %copy-start.2 = (bf16[1,256,512]{2,1,0:T(8,128)(2,1)S(1)}, bf16[1,256,512]{2,1,0:T(8,128)(2,1)}, u32[]{:S(2)}) copy-start(bf16[1,256,512]{2,1,0:T(8,128)(2,1)} %refs_2_.1) | copy-start | bytes 786436
  3.7 0.9 %copy-start.3 = (bf16[1,256,512]{2,1,0:T(8,128)(2,1)S(1)}, bf16[1,256,512]{2,1,0:T(8,128)(2,1)}, u32[]{:S(2)}) copy-start(bf16[1,256,512]{2,1,0:T(8,128)(2,1)} %refs_3_.1) | copy-start | bytes 786436
  4.6 0.9 %copy-start.4 = (bf16[256,512]{1,0:T(8,128)(2,1)S(1)}, bf16[256,512]{1,0:T(8,128)(2,1)}, u32[]{:S(2)}) copy-start(bf16[256,512]{1,0:T(8,128)(2,1)} %refs_4_.1) | copy-start | bytes 786436

commit v3 on v2

--- a/solution.py
+++ b/solution.py
@@ -193,6 +193,10 @@
     loads[6].wait()
     first(h)
 
+    for i in range(2):
+        stored_l[i] = complex_square(less_ref[i])
+        stored_g[i] = complex_square(great_ref[i])
+
     def scatter(k, u):
         g = lax.rem(q + k, nq)
         return remote(pre.at[k, u], rs_in.at[k, u], rs_s.at[k, u], rs_r.at[k, u], tp=2 * g + h)
@@ -208,10 +212,6 @@
                 launch(scatter(k, u))
             else:
                 kept.append(total)
-
-    for i in range(2):
-        stored_l[i] = complex_square(less_ref[i])
-        stored_g[i] = complex_square(great_ref[i])
 
     def gather(k, u):
         g = lax.rem(q + k, nq)
@@ -374,7 +374,7 @@
             + [dma((nq, nu))] * 8
             + [dma((npair, nu))] * 8,
             compiler_params=pltpu.CompilerParams(
-                collective_id=0, has_side_effects=True, vmem_limit_bytes=48 * 1024 * 1024
+                collective_id=0, has_side_effects=True, vmem_limit_bytes=63 * 1024 * 1024 + 512 * 1024
             ),
             name="advance",
         )(less, great, rowl, rowg, prop)

time: 51 us -> 47.3 us (0.927)
  local copies, waits for them, and re-layouts: 6.33 us -> 2.42 us
    unnamed x12 -> x4, local copies, waits for them, and re-layouts: 6.33 us -> 2.42 us
where the time goes in v3:
time: 47.3 us; the launch traced here: 47.1 us
  Pallas kernels  44 us (93%)
  local copies, waits for them, and re-layouts  2.42 us (5%)
  between operations  0.65 us (1%)
    pallas_call x1, Pallas kernels, local(): pl.pallas_call(lambda *refs: kernel(na, nt, nu, *refs), out_shape=(out, o...  44 us
    unnamed x4, local copies, waits for them, and re-layouts  2.42 us

profile of v3, /device:TPU:0, one launch (start us, length us, event | category | flops | bytes accessed | tf_op | source)
XLA Modules:
  0.0 47.1 jit_solution(16649554552144455916)
XLA Ops:
  0.6 44.0 %advance.1 = (bf16[1,256,512]{2,1,0:T(8,128)(2,1)}, bf16[1,256,512]{2,1,0:T(8,128)(2,1)}) custom-call(bf16[2,1,256,512]{3,2,1,0:T(8,128)(2,1)} %refs_0_.1, bf16[2,1,256,512]{3,2,1,0:T(8,128)(2,1)} %refs_1_.1, bf16[1,256,512]{2,1,0:T(8,128)(2,1)} %refs_2_.1, bf16[1,256,512]{2,1,0:T(8,128)(2,1)} %refs_3_.1, bf16[256,512]{1,0:T(8,128)(2,1)} %refs_4_.1), custom_call_target="tpu_custom_call" | custom-call | tf_op jit(solution)/shard_map/advance/pallas_call | solution.py:350
  44.7 0.0 copy-start
  44.7 1.7 %copy.9 = bf16[1,256,512]{2,1,0:T(8,128)(2,1)} copy(bf16[1,256,512]{2,1,0:T(8,128)(2,1)} %get-tuple-element.4) | data formatting | bytes 524288
  46.4 0.0 copy-done
  46.4 0.7 %copy.10 = bf16[1,256,512]{2,1,0:T(8,128)(2,1)} copy(bf16[1,256,512]{2,1,0:T(8,128)(2,1)S(1)} %copy-done) | data formatting | bytes 524288
Async XLA Ops:
  44.7 1.7 %copy-start = (bf16[1,256,512]{2,1,0:T(8,128)(2,1)S(1)}, bf16[1,256,512]{2,1,0:T(8,128)(2,1)}, u32[]{:S(2)}) copy-start(bf16[1,256,512]{2,1,0:T(8,128)(2,1)} %get-tuple-element.5) | copy-start | bytes 786436

commit v4 on v3

--- a/solution.py
+++ b/solution.py
@@ -313,6 +313,7 @@
         for k in range(1, npair):
             z_gather(k, u).wait_recv()
             launch(z_forward(k, u, ha))
+    for u in range(nu):
         for k in range(npair):
             z_forward(k, u, 1 - ha).wait_recv()
         at = u * wu

time: 47.3 us -> 47 us (level)
  no operation moved by 1% of the time
where the time goes in v4:
time: 47 us; the launch traced here: 46.8 us
  Pallas kernels  43.7 us (93%)
  local copies, waits for them, and re-layouts  2.42 us (5%)
  between operations  0.65 us (1%)
    pallas_call x1, Pallas kernels, local(): pl.pallas_call(lambda *refs: kernel(na, nt, nu, *refs), out_shape=(out, o...  43.7 us
    unnamed x4, local copies, waits for them, and re-layouts  2.42 us

profile of v4, /device:TPU:0, one launch (start us, length us, event | category | flops | bytes accessed | tf_op | source)
XLA Modules:
  0.0 46.8 jit_solution(1696236136176434056)
XLA Ops:
  0.6 43.7 %advance.1 = (bf16[1,256,512]{2,1,0:T(8,128)(2,1)}, bf16[1,256,512]{2,1,0:T(8,128)(2,1)}) custom-call(bf16[2,1,256,512]{3,2,1,0:T(8,128)(2,1)} %refs_0_.1, bf16[2,1,256,512]{3,2,1,0:T(8,128)(2,1)} %refs_1_.1, bf16[1,256,512]{2,1,0:T(8,128)(2,1)} %refs_2_.1, bf16[1,256,512]{2,1,0:T(8,128)(2,1)} %refs_3_.1, bf16[256,512]{1,0:T(8,128)(2,1)} %refs_4_.1), custom_call_target="tpu_custom_call" | custom-call | tf_op jit(solution)/shard_map/advance/pallas_call | solution.py:351
  44.4 0.0 copy-start
  44.4 1.7 %copy.9 = bf16[1,256,512]{2,1,0:T(8,128)(2,1)} copy(bf16[1,256,512]{2,1,0:T(8,128)(2,1)} %get-tuple-element.4) | data formatting | bytes 524288
  46.1 0.0 copy-done
  46.1 0.7 %copy.10 = bf16[1,256,512]{2,1,0:T(8,128)(2,1)} copy(bf16[1,256,512]{2,1,0:T(8,128)(2,1)S(1)} %copy-done) | data formatting | bytes 524288
Async XLA Ops:
  44.4 1.7 %copy-start = (bf16[1,256,512]{2,1,0:T(8,128)(2,1)S(1)}, bf16[1,256,512]{2,1,0:T(8,128)(2,1)}, u32[]{:S(2)}) copy-start(bf16[1,256,512]{2,1,0:T(8,128)(2,1)} %get-tuple-element.5) | copy-start | bytes 786436
